TPU v7x, 32 devices: a whole 2x2x4 slice. The times are simulated.
32 devices in a mesh: grp: 4 (over z), wide: 8 (over y, x, core).
Axes of the slice: x: 2, y: 2, z: 4, core: 2. Of those that a mesh axis runs over, the one named last changes fastest.
Arguments:
- half_integrals: bfloat16 [8, 4, 1024, 2048], P('wide', None, None, 'grp'), may hold values from -0.47851562 to 0.47851562
- coeff_virtual: bfloat16 [1024, 768], replicated, may hold values from -0.1875 to 0.1875
- occ_energy: float32 [8, 4], replicated, may hold values from -2 to -0.3
- vir_energy: float32 [768], replicated, may hold values from 0.2 to 3
- plan: int32 [2, 2], replicated, may hold values from 0 to 7, as said below
Outputs:
- density_three: float32 [8, 4, 768, 2048], P('wide', 'grp')
Inputs may be any that keep to these rules, and one draw needn't show every extreme that they name: plan[s, k] is the owner block whose orbitals serve step s, slot k; the value 0 and the value 8 - 1 both occur in every draw, an owner may repeat.
All inputs are finite; a program needn't handle non-finite values.
Results may differ from a plain program's by a relative error of at most 0.0039.
Values may be sent and summed in bfloat16 or wider, within the bound.
A program may use at most 128 MiB of HBM per device.

v0:
```python
import jax
import jax.numpy as jnp
from jax import lax
from jax.sharding import PartitionSpec as P

STEPS = 2


def from_root(value, axis, source):
    kept = jnp.where(lax.axis_index(axis) == source, value, 0).astype(value.dtype)
    return lax.psum(kept, axis)


def pair_terms(rows_i, rows_j, energy_i, energy_j, vir_energy):
    intersection = jnp.einsum("iap,jbp->ijab", rows_i, rows_j, preferred_element_type=jnp.float32)
    denominator = (
        energy_i[:, None, None, None]
        + energy_j[None, :, None, None]
        - vir_energy[None, None, :, None]
        - vir_energy[None, None, None, :]
    )
    amplitude = intersection / denominator
    combined = (2.0 * amplitude - jnp.swapaxes(amplitude, 2, 3)).astype(jnp.bfloat16)
    return jnp.einsum("ijab,jbp->iap", combined, rows_j, preferred_element_type=jnp.float32)


def shards(half_integrals, coeff_virtual, occ_energy, vir_energy, plan):
    transformed = jnp.einsum(
        "wimp,ma->wiap", half_integrals, coeff_virtual, preferred_element_type=jnp.float32
    ).astype(jnp.bfloat16)
    owned = lax.all_to_all(transformed, "grp", split_axis=1, concat_axis=3, tiled=True)
    owned_rows = owned[0]
    per_dev = owned_rows.shape[0]
    group_start = lax.axis_index("grp") * per_dev
    mine_energy = lax.dynamic_slice(
        occ_energy, (lax.axis_index("wide"), group_start), (1, per_dev)
    )[0]
    density = jnp.zeros(owned_rows.shape, jnp.float32)
    for step_index in range(STEPS):
        for slot_index in range(2):
            owner_index = plan[step_index, slot_index]
            remote_rows = from_root(owned_rows, "wide", owner_index)
            remote_energy = lax.dynamic_slice(occ_energy, (owner_index, group_start), (1, per_dev))[
                0
            ]
            density = density + pair_terms(
                owned_rows, remote_rows, mine_energy, remote_energy, vir_energy
            )
    return density[None]


def solution(mesh):
    return jax.shard_map(
        shards,
        mesh=mesh,
        in_specs=(P("wide", None, None, "grp"), P(), P(), P(), P()),
        out_specs=P("wide", "grp", None, None),
        check_vma=False,
    )
```

profile of v0, /device:TPU:0, one launch (start us, length us, event | category | flops | bytes accessed | tf_op | source)
XLA Modules:
  0.0 351.6 jit_solution(16205879128177095437)
XLA Ops:
  6.5 1.4 copy-done
  7.9 7.0 %convert_bitcast_fusion = bf16[1,4,768,512]{3,2,0,1:T(8,128)(2,1)} fusion(bf16[1,4,1024,512]{3,2,1,0:T(8,128)(2,1)} %param.5, bf16[1024,768]{1,0:T(8,128)(2,1)S(1)} %copy-done), kind=kOutput, calls=%fused_computation.7 | convolution fusion | flops 3222798336 | bytes 8912896 | tf_op jit(solution)/shard_map/wimp,ma->wiap/dot_general | solution.py:28
  15.0 6.5 %all-to-all-start = ((bf16[1,4,768,512]{3,2,0,1:T(8,128)(2,1)}), bf16[1,4,768,512]{3,2,0,1:T(8,128)(2,1)S(1)}, u32[]{:S(2)}, u32[]{:S(2)}) async-start(bf16[1,4,768,512]{3,2,0,1:T(8,128)(2,1)} %convert_bitcast_fusion), calls=%async_computation | async-start | bytes 6291456 | tf_op jit(solution)/shard_map/all_to_all | solution.py:31
  21.4 0.6 fusion.29
  24.5 67.6 %all-to-all-done = bf16[1,4,768,512]{3,2,0,1:T(8,128)(2,1)S(1)} async-done(((bf16[1,4,768,512]{3,2,0,1:T(8,128)(2,1)}), bf16[1,4,768,512]{3,2,0,1:T(8,128)(2,1)S(1)}, u32[]{:S(2)}, u32[]{:S(2)}) %all-to-all-start) | async-done | bytes 3145760 | tf_op jit(solution)/shard_map/all_to_all | solution.py:31
  92.1 2.8 copy.23
  94.8 6.1 %bitcast_select_fusion.2 = (bf16[1,1,768,4,512]{2,4,3,1,0:T(8,128)(2,1)}, bf16[1,1,768,4,512]{2,4,3,1,0:T(8,128)(2,1)}, bf16[1,1,768,4,512]{2,4,3,1,0:T(8,128)(2,1)}, bf16[1,1,768,4,512]{2,4,3,1,0:T(8,128)(2,1)}) fusion(bf16[1,4,768,512]{2,3,1,0:T(8,128)(2,1)} %copy.23, pred[]{:T(512)S(6)} %eq.15, pred[]{:T(512)S(6)} %eq.13, pred[]{:T(512)S(6)} %eq.14, ...), kind=kLoop, calls=%fused_computation.5 | loop fusion | flops 6291456 | bytes 15728644 | tf_op jit(solution)/shard_map/jit(_where)/select_n | solution.py:10
  100.9 0.0 all-reduce.3.cloned.1.call-update
  108.7 0.7 fusion.28
  114.1 0.0 copy-done.5
  114.1 159.5 %all-reduce.3.cloned.1.call-done = (bf16[768,2048]{0,1:T(8,128)(2,1)}, bf16[768,2048]{0,1:T(8,128)(2,1)}, bf16[768,2048]{0,1:T(8,128)(2,1)}, bf16[768,2048]{0,1:T(8,128)(2,1)}) async-done(((bf16[768,2048]{0,1:T(8,128)(2,1)}, bf16[768,2048]{0,1:T(8,128)(2,1)}, bf16[768,2048]{0,1:T(8,128)(2,1)}, bf16[768,2048]{0,1:T(8,128)(2,1)}), (bf16[768,2048]{0,1:T(8,128)(2,1)}, bf16[768,2048]{0,1:T(8,128)(2,1)}, ...) | async-done | bytes 12582928 | tf_op jit(solution)/shard_map/psum | solution.py:11
  273.6 0.0 copy-done.2
  273.6 6.0 %bitcast_divide_fusion.1 = f32[1,1,768,768]{2,3,0,1:T(8,128)} fusion(bf16[768,2048]{0,1:T(8,128)(2,1)} %get-tuple-element.5, bf16[768,2048]{0,1:T(8,128)(2,1)S(1)} %bitcast.105, f32[768]{0:T(1024)S(1)} %get-tuple-element.16, f32[768]{0:T(1024)S(1)} %copy-done.5), kind=kOutput, calls=%fused_computation.9 | convolution fusion | flops 2417098752 | bytes 8656896 | tf_op jit(solution)/shard_map/iap,jbp->ijab/dot_general | solution.py:15
  279.6 3.1 copy.26
  282.7 8.8 %fusion.16 = f32[768,2048]{1,0:T(8,128)} fusion(bf16[768,2048]{0,1:T(8,128)(2,1)} %get-tuple-element.5, f32[1,1,768,768]{2,3,0,1:T(8,128)} %bitcast_divide_fusion.1, f32[1,1,768,768]{3,2,0,1:T(8,128)} %copy.26), kind=kOutput, calls=%fused_computation.26 | convolution fusion | flops 2417688576 | bytes 14155776 | tf_op jit(solution)/shard_map/ijab,jbp->iap/dot_general | solution.py:24
  291.5 4.1 %bitcast_divide_fusion.3 = f32[1,1,768,768]{2,3,0,1:T(8,128)} fusion(bf16[768,2048]{0,1:T(8,128)(2,1)S(1)} %copy-done.8, bf16[768,2048]{0,1:T(8,128)(2,1)S(1)} %bitcast.106, f32[768]{0:T(1024)S(1)} %copy-done.5, f32[768]{0:T(1024)S(1)} %get-tuple-element.15), kind=kOutput, calls=%fused_computation.11 | convolution fusion | flops 2417098752 | bytes 8656896 | tf_op jit(solution)/shard_map/iap,jbp->ijab/dot_general | solution.py:15
  295.6 3.0 copy.24
  298.6 8.8 %fusion.10 = f32[768,2048]{1,0:T(8,128)} fusion(bf16[768,2048]{0,1:T(8,128)(2,1)} %get-tuple-element.6, f32[1,1,768,768]{2,3,0,1:T(8,128)} %bitcast_divide_fusion.3, f32[1,1,768,768]{3,2,0,1:T(8,128)} %copy.24), kind=kOutput, calls=%fused_computation.22 | convolution fusion | flops 2417688576 | bytes 14155776 | tf_op jit(solution)/shard_map/ijab,jbp->iap/dot_general | solution.py:24
  307.4 4.1 %bitcast_divide_fusion.2 = f32[1,1,768,768]{2,3,0,1:T(8,128)} fusion(bf16[768,2048]{0,1:T(8,128)(2,1)S(1)} %copy-done.7, bf16[768,2048]{0,1:T(8,128)(2,1)S(1)} %bitcast.107, f32[768]{0:T(1024)S(1)} %get-tuple-element.14, f32[768]{0:T(1024)S(1)} %copy-done.5), kind=kOutput, calls=%fused_computation.10 | convolution fusion | flops 2417098752 | bytes 8656896 | tf_op jit(solution)/shard_map/iap,jbp->ijab/dot_general | solution.py:15
  311.5 3.1 copy.25
  314.6 8.7 %fusion.13 = f32[768,2048]{1,0:T(8,128)} fusion(bf16[768,2048]{0,1:T(8,128)(2,1)} %get-tuple-element.7, f32[1,1,768,768]{2,3,0,1:T(8,128)} %bitcast_divide_fusion.2, f32[1,1,768,768]{3,2,0,1:T(8,128)} %copy.25), kind=kOutput, calls=%fused_computation.24 | convolution fusion | flops 2417688576 | bytes 14155776 | tf_op jit(solution)/shard_map/ijab,jbp->iap/dot_general | solution.py:24
  323.3 4.1 %bitcast_divide_fusion = f32[1,1,768,768]{2,3,0,1:T(8,128)} fusion(bf16[768,2048]{0,1:T(8,128)(2,1)S(1)} %copy-done.3, bf16[768,2048]{0,1:T(8,128)(2,1)S(1)} %bitcast.108, f32[768]{0:T(1024)S(1)} %get-tuple-element.13, f32[768]{0:T(1024)S(1)} %copy-done.5), kind=kOutput, calls=%fused_computation.8 | convolution fusion | flops 2417098752 | bytes 8656896 | tf_op jit(solution)/shard_map/iap,jbp->ijab/dot_general | solution.py:15
  327.5 3.1 copy.27
  330.5 14.2 %add_bitcast_fusion = f32[1,1,768,2048]{3,2,1,0:T(8,128)} fusion(f32[768,2048]{1,0:T(8,128)} %fusion.16, f32[768,2048]{1,0:T(8,128)} %fusion.10, f32[768,2048]{1,0:T(8,128)} %fusion.13, bf16[768,2048]{0,1:T(8,128)(2,1)} %get-tuple-element.8, f32[1,1,768,768]{2,3,0,1:T(8,128)} %bitcast_divide_fusion, f32[1,1,768,768]{3,2,0,1:T(8,128)} %copy.27), kind=kOutput, calls=%fused_computation | convolution fusion | flops 2422407168 | bytes 33030144 | tf_op jit(solution)/shard_map/ijab,jbp->iap/dot_general | solution.py:24
  (17 shorter events, 0.0 us)
Async XLA Ops:
  6.5 1.4 copy-start
  15.0 6.5 %copy-start.4 = (s32[2,2]{1,0:T(2,128)S(1)}, s32[2,2]{1,0:T(2,128)}, u32[]{:S(2)}) copy-start(s32[2,2]{1,0:T(2,128)} %param.9) | copy-start | bytes 52
  15.0 77.1 %all-to-all-start = ((bf16[1,4,768,512]{3,2,0,1:T(8,128)(2,1)}), bf16[1,4,768,512]{3,2,0,1:T(8,128)(2,1)S(1)}, u32[]{:S(2)}, u32[]{:S(2)}) async-start(bf16[1,4,768,512]{3,2,0,1:T(8,128)(2,1)} %convert_bitcast_fusion), calls=%async_computation | async-start | bytes 6291456 | tf_op jit(solution)/shard_map/all_to_all | solution.py:31
  21.4 252.2 %all-reduce.3.cloned.1.call-start = ((), (), s32[]{:S(2)}) async-start(), calls=%async_computation.1 | async-start | bytes 25165824 | tf_op jit(solution)/shard_map/psum | solution.py:11
  100.9 7.8 %copy-start.6 = (f32[8,4]{0,1:T(4,128)S(1)}, f32[8,4]{0,1:T(4,128)}, u32[]{:S(2)}) copy-start(f32[8,4]{0,1:T(4,128)} %param.7) | copy-start | bytes 388
  100.9 13.2 %copy-start.5 = (f32[768]{0:T(1024)S(1)}, f32[768]{0:T(1024)}, u32[]{:S(2)}) copy-start(f32[768]{0:T(1024)} %param.8) | copy-start | bytes 9220
  100.9 172.7 %copy-start.2 = (bf16[1,4,768,512]{2,3,1,0:T(8,128)(2,1)S(1)}, bf16[1,4,768,512]{2,3,1,0:T(8,128)(2,1)}, u32[]{:S(2)}) copy-start(bf16[1,4,768,512]{2,3,1,0:T(8,128)(2,1)} %copy.23) | copy-start | bytes 9437188
  282.7 8.8 %copy-start.8 = (bf16[768,2048]{0,1:T(8,128)(2,1)S(1)}, bf16[768,2048]{0,1:T(8,128)(2,1)}, u32[]{:S(2)}) copy-start(bf16[768,2048]{0,1:T(8,128)(2,1)} %get-tuple-element.6) | copy-start | bytes 9437188
  298.6 8.8 %copy-start.7 = (bf16[768,2048]{0,1:T(8,128)(2,1)S(1)}, bf16[768,2048]{0,1:T(8,128)(2,1)}, u32[]{:S(2)}) copy-start(bf16[768,2048]{0,1:T(8,128)(2,1)} %get-tuple-element.7) | copy-start | bytes 9437188
  314.6 8.7 %copy-start.3 = (bf16[768,2048]{0,1:T(8,128)(2,1)S(1)}, bf16[768,2048]{0,1:T(8,128)(2,1)}, u32[]{:S(2)}) copy-start(bf16[768,2048]{0,1:T(8,128)(2,1)} %get-tuple-element.8) | copy-start | bytes 9437188
  330.5 14.2 %copy-start.1 = (bf16[1024,768]{1,0:T(8,128)(2,1)S(1)}, bf16[1024,768]{1,0:T(8,128)(2,1)}, u32[]{:S(2)}) copy-start(bf16[1024,768]{1,0:T(8,128)(2,1)} %param.6) | copy-start | bytes 4718596
Sparse Core Ops, SparseCore 0:
  101.1 172.4 all-reduce.2
where the time goes:
time: 352 us
  waiting for transfers between devices  227 us (64%)
  matrix products  65.9 us (19%)
  between operations  28.4 us (8%)
  local copies, waits for them, and re-layouts  17.7 us (5%)
  starting transfers between devices  6.45 us (2%)
  other arithmetic  6.08 us (2%)
    psum x1, waiting for transfers between devices, from_root(): return lax.psum(kept, axis)  159 us
    all_to_all x1, waiting for transfers between devices, shards(): lax.all_to_all(transformed, 'grp', split_axis=1, concat_axis=3, tiled=True)  67.6 us
    dot_general x4, matrix products, pair_terms(): jnp.einsum('ijab,jbp->iap', combined, rows_j, preferred_element_type=jnp....  40.5 us
    dot_general x4, matrix products, pair_terms(): jnp.einsum('iap,jbp->ijab', rows_i, rows_j, preferred_element_type=jnp.fl...  18.4 us
    div x4, local copies, waits for them, and re-layouts, pair_terms(): amplitude = intersection / denominator  12.2 us
  transfers between devices with their start and end apart: 2, of which 2 were waited for; matrix products, arithmetic and copies ran while one was open for 0% of the time, Pallas kernels for 0%

commit v1 on v0

v1 whole, which is shorter than its diff:
```python
import functools

import jax
import jax.numpy as jnp
from jax import lax
from jax.experimental import pallas as pl
from jax.experimental.pallas import tpu as pltpu
from jax.sharding import PartitionSpec as P

MESH = pl.DeviceIdType.MESH


def kernel(
    n_grp, n_wide, slots, paths,
    owners, energy, trans, vir_col, vir_row,
    out,
    mine, sib, near, msg, far, owned, acc, comb, stage,
    local_sem, a2a_s, a2a_r, sib_s, sib_r, near_s, near_r, msg_s, msg_r, own_s, own_r, out_sem,
):
    g = lax.axis_index("grp")
    w = lax.axis_index("wide")
    virt, pb = mine.shape[1], mine.shape[2]
    half = virt // 2
    rb = half // paths
    bits = n_wide.bit_length() - 2
    core = lax.rem(w, 2)
    my_half = pl.multiple_of(core * half, 16)
    sib_half = pl.multiple_of((1 - core) * half, 16)

    def flip(index, bit):
        size = 1 << bit
        return index + size - 2 * size * lax.rem(lax.div(index, size), 2)

    def flip_grp(k):
        index = g
        for bit in range(n_grp.bit_length() - 1):
            if (k >> bit) & 1:
                index = flip(index, bit)
        return index

    def step_bit(h, t):
        return 1 + (h + t) % bits

    def remote(src, dst, send, recv, **device):
        return pltpu.make_async_remote_copy(
            src_ref=src, dst_ref=dst, send_sem=send, recv_sem=recv,
            device_id=device, device_id_type=MESH,
        )

    barrier = pltpu.get_barrier_semaphore()
    for bit in range(bits + 1):
        pl.semaphore_signal(
            barrier, inc=1, device_id={"wide": flip(w, bit)}, device_id_type=MESH
        )
    for k in range(1, n_grp):
        pl.semaphore_signal(
            barrier, inc=1, device_id={"grp": flip_grp(k)}, device_id_type=MESH
        )
    pl.semaphore_wait(barrier, bits + n_grp)

    sent = []

    def go(copy):
        copy.start()
        sent.append(copy)
        return copy

    a2a = [None]
    for k in range(1, n_grp):
        peer = flip_grp(k)
        a2a.append(go(remote(trans.at[peer], mine.at[k], a2a_s.at[k], a2a_r.at[k], grp=peer)))
    local = pltpu.make_async_copy(trans.at[g], mine.at[0], local_sem)
    local.start()
    local.wait()

    near_in, msg_in, own_in = {}, {}, {}

    def exchange_near(k):
        if k:
            a2a[k].wait_recv()
        pair = go(remote(
            mine.at[k, pl.ds(sib_half, half)], sib.at[k], sib_s.at[k], sib_r.at[k], wide=flip(w, 0)
        ))
        for h in range(paths):
            peer = flip(w, step_bit(h, 0))
            rows = pl.ds(pl.multiple_of(my_half + h * rb, 16), rb)
            near_in[k, h, 0] = go(remote(
                mine.at[k, rows], near.at[k, h, 0], near_s.at[k, h, 0], near_r.at[k, h, 0], wide=peer
            ))
        pair.wait_recv()
        for h in range(paths):
            peer = flip(w, step_bit(h, 0))
            near_in[k, h, 1] = go(remote(
                sib.at[k, pl.ds(h * rb, rb)], near.at[k, h, 1],
                near_s.at[k, h, 1], near_r.at[k, h, 1], wide=peer,
            ))

    def same(owner, index):
        return owner == index

    def in_far(owner, h, t):
        inside = [0] + [step_bit(h, u) for u in range(t)]
        there = flip(w, step_bit(h, t))
        ok = None
        for bit in range(bits + 1):
            if bit in inside:
                continue
            agree = lax.rem(lax.div(owner, 1 << bit), 2) == lax.rem(lax.div(there, 1 << bit), 2)
            ok = agree if ok is None else jnp.logical_and(ok, agree)
        return ok

    def pick(k, h, t, r, who, unit):
        rows = 32 if rb % 32 == 0 else 16
        at = pl.multiple_of(r * rows, rows)
        value = mine[k, pl.ds(pl.multiple_of(my_half + h * rb + at, 16), rows), :]
        first = flip(w, step_bit(h, 0))
        choices = [
            (flip(w, 0), lambda: sib[k, pl.ds(pl.multiple_of(h * rb + at, 16), rows), :]),
            (first, lambda: near[k, h, 0, pl.ds(at, rows), :]),
            (flip(first, 0), lambda: near[k, h, 1, pl.ds(at, rows), :]),
        ]
        for index, load in choices:
            for owner in who:
                value = lax.select(same(owner, index), load(), value)
        for u in range(1, t):
            for owner in who:
                value = lax.select(
                    in_far(owner, h, u), far[k, h, u - 1, unit, pl.ds(at, rows), :], value
                )
        return value

    def row_loop(body):
        rows = 32 if rb % 32 == 0 else 16

        @pl.loop(0, rb // rows)
        def _(r):
            body(r, pl.multiple_of(r * rows, rows), rows)

    def exchange_far(k, t):
        for h in range(paths):
            if t == 1:
                near_in[k, h, 0].wait_recv()
                near_in[k, h, 1].wait_recv()
            else:
                msg_in[k, h, t - 1].wait_recv()

            def body(r, at, rows):
                for unit in range(slots - 1):
                    who = [0, n_wide - 1] if unit == 0 else [owners[unit]]
                    msg[k, h, t - 1, unit, pl.ds(at, rows), :] = pick(k, h, t, r, who, unit)

            row_loop(body)
            msg_in[k, h, t] = go(remote(
                msg.at[k, h, t - 1], far.at[k, h, t - 1],
                msg_s.at[k, h, t - 1], msg_r.at[k, h, t - 1], wide=flip(w, step_bit(h, t)),
            ))

    def to_sibling(k):
        for h in range(paths):
            msg_in[k, h, bits - 1].wait_recv()

            def body(r, at, rows):
                for s in range(slots):
                    unit = 0 if s in (0, slots - 1) else s
                    who = {0: 0, slots - 1: n_wide - 1}.get(s)
                    who = owners[s] if who is None else who
                    owned[k, s, pl.ds(pl.multiple_of(my_half + h * rb + at, 16), rows), :] = pick(
                        k, h, bits, r, [who], unit
                    )

            row_loop(body)
        part = owned.at[k, :, pl.ds(my_half, half), :]
        own_in[k] = go(remote(part, part, own_s.at[k], own_r.at[k], wide=flip(w, 0)))

    tile = 256 if virt % 256 == 0 else virt
    contract = (((1,), (1,)), ((), ()))

    def intersect(k):
        own_in[k].wait_recv()

        @pl.loop(0, slots)
        def _(s):
            @pl.loop(0, virt // tile)
            def _(r):
                rows = pl.ds(pl.multiple_of(r * tile, tile), tile)
                straight = lax.dot_general(
                    mine[k, rows, :], owned[k, s], contract, preferred_element_type=jnp.float32
                )
                turned = lax.dot_general(
                    owned[k, s, rows, :], mine[k], contract, preferred_element_type=jnp.float32
                )
                value = 2.0 * straight - turned
                if k:
                    value = value + acc[s, rows, :]
                acc[s, rows, :] = value

    exchange_near(0)
    for t in range(1, bits):
        exchange_far(0, t)
    for k in range(n_grp):
        if k + 1 < n_grp:
            exchange_near(k + 1)
        to_sibling(k)
        if k + 1 < n_grp:
            for t in range(1, bits):
                exchange_far(k + 1, t)
        intersect(k)

    for s in range(slots):
        total = energy[s]

        @pl.loop(0, virt // tile)
        def _(r):
            rows = pl.ds(pl.multiple_of(r * tile, tile), tile)
            denominator = (total - vir_col[rows, :]) - vir_row[...]
            comb[rows, pl.ds(s * virt, virt)] = (acc[s, rows, :] / denominator).astype(jnp.bfloat16)

    outs = []
    for k in range(n_grp):
        if k >= 2:
            outs[k - 2].wait()

        @pl.loop(0, virt // tile)
        def _(r):
            rows = pl.ds(pl.multiple_of(r * tile, tile), tile)
            stage[k % 2, rows, :] = jnp.dot(
                comb[rows, :], owned[k].reshape(slots * virt, pb),
                preferred_element_type=jnp.float32,
            )

        columns = pl.ds(pl.multiple_of(flip_grp(k) * pb, 128), pb)
        copy = pltpu.make_async_copy(stage.at[k % 2], out.at[:, columns], out_sem.at[k % 2])
        copy.start()
        outs.append(copy)
    for copy in outs[-2:]:
        copy.wait()
    for copy in sent:
        copy.wait_send()


def shards(n_grp, n_wide, half_integrals, coeff_virtual, occ_energy, vir_energy, plan):
    trans = jnp.einsum(
        "imp,ma->iap", half_integrals[0], coeff_virtual, preferred_element_type=jnp.float32
    ).astype(jnp.bfloat16)
    virt, pb = trans.shape[1:]
    owners = jnp.sort(plan.reshape(-1))
    slots = owners.shape[0]
    orbital = lax.axis_index("grp")
    energy = occ_energy[lax.axis_index("wide"), orbital] + occ_energy[owners, orbital]
    bits = n_wide.bit_length() - 2
    paths = bits if virt % (32 * bits) == 0 else 1
    rb = virt // 2 // paths
    bf16, f32 = jnp.bfloat16, jnp.float32
    dma = pltpu.SemaphoreType.DMA
    smem = pl.BlockSpec(memory_space=pltpu.SMEM)
    vmem = pl.BlockSpec(memory_space=pltpu.VMEM)
    hbm = pl.BlockSpec(memory_space=pl.ANY)
    flops = 3 * 2 * slots * virt * virt * pb * n_grp
    density = pl.pallas_call(
        functools.partial(kernel, n_grp, n_wide, slots, paths),
        out_shape=jax.ShapeDtypeStruct((virt, pb * n_grp), f32),
        in_specs=[smem, smem, hbm, vmem, vmem],
        out_specs=hbm,
        scratch_shapes=[
            pltpu.VMEM((n_grp, virt, pb), bf16),
            pltpu.VMEM((n_grp, virt // 2, pb), bf16),
            pltpu.VMEM((n_grp, paths, 2, rb, pb), bf16),
            pltpu.VMEM((n_grp, paths, bits - 1, slots - 1, rb, pb), bf16),
            pltpu.VMEM((n_grp, paths, bits - 1, slots - 1, rb, pb), bf16),
            pltpu.VMEM((n_grp, slots, virt, pb), bf16),
            pltpu.VMEM((slots, virt, virt), f32),
            pltpu.VMEM((virt, slots * virt), bf16),
            pltpu.VMEM((2, virt, pb), f32),
            dma(()),
            dma((n_grp,)), dma((n_grp,)),
            dma((n_grp,)), dma((n_grp,)),
            dma((n_grp, paths, 2)), dma((n_grp, paths, 2)),
            dma((n_grp, paths, bits - 1)), dma((n_grp, paths, bits - 1)),
            dma((n_grp,)), dma((n_grp,)),
            dma((2,)),
        ],
        compiler_params=pltpu.CompilerParams(
            collective_id=0, has_side_effects=True, vmem_limit_bytes=63 * 1024 * 1024
        ),
        cost_estimate=pl.CostEstimate(
            flops=flops, bytes_accessed=16 * virt * pb * n_grp, transcendentals=0
        ),
    )(owners, energy, trans, vir_energy[:, None], vir_energy[None, :])
    return density[None, None]


def solution(mesh):
    return jax.shard_map(
        functools.partial(shards, mesh.shape["grp"], mesh.shape["wide"]),
        mesh=mesh,
        in_specs=(P("wide", None, None, "grp"), P(), P(), P(), P()),
        out_specs=P("wide", "grp", None, None),
        check_vma=False,
    )
```

time: 352 us -> 159 us (0.45)
  waiting for transfers between devices: 227 us -> 0 us
  Pallas kernels: 0 us -> 133 us
  matrix products: 65.9 us -> 7.79 us
  between operations: 28.4 us -> 0.02 us
  starting transfers between devices: 6.45 us -> 0 us
  local copies, waits for them, and re-layouts: 17.7 us -> 12.6 us
  other arithmetic: 6.08 us -> 2.01 us
    psum x1 -> x0, waiting for transfers between devices: 159 us -> none  [from_root(): return lax.psum(kept, axis)]
    pallas_call x0 -> x1, Pallas kernels: none -> 133 us  [shards(): pl.pallas_call(functools.partial(kernel, n_grp, n_wide, slots, paths), ou...]
    all_to_all x1 -> x0, waiting for transfers between devices: 67.6 us -> none  [shards(): lax.all_to_all(transformed, 'grp', split_axis=1, concat_axis=3, tiled=True)]
    dot_general x9 -> x1, matrix products: 65.9 us -> 7.79 us  [shards(): jnp.einsum('imp,ma->iap', half_integrals[0], coeff_virtual, preferred_ele...]
    div x4 -> x0, local copies, waits for them, and re-layouts: 12.2 us -> none  [pair_terms(): amplitude = intersection / denominator]
    all_to_all x1 -> x0, starting transfers between devices: 6.45 us -> none  [shards(): lax.all_to_all(transformed, 'grp', split_axis=1, concat_axis=3, tiled=True)]
    select_n x1 -> x0, other arithmetic: 6.07 us -> none  [from_root(): jnp.where(lax.axis_index(axis) == source, value, 0).astype(value.dtype)]
    unnamed x18 -> x3, local copies, waits for them, and re-layouts: 1.44 us -> 6.29 us
  transfers between devices with their start and end apart: 2 -> 0, of which waited for: 2 -> 0; matrix products, arithmetic and copies ran while one was open for 0% -> 0% of each run, Pallas kernels for 0% -> 0%
where the time goes in v1:
time: 159 us; the launch traced here: 156 us
  Pallas kernels  133 us (84%)
  local copies, waits for them, and re-layouts  12.6 us (8%)
  matrix products  7.79 us (5%)
  other arithmetic  2.01 us (1%)
    pallas_call x1, Pallas kernels, shards(): pl.pallas_call(functools.partial(kernel, n_grp, n_wide, slots, paths), ou...  133 us
    dot_general x1, matrix products, shards(): jnp.einsum('imp,ma->iap', half_integrals[0], coeff_virtual, preferred_ele...  7.79 us
    unnamed x3, local copies, waits for them, and re-layouts  6.29 us

profile of v1, /device:TPU:0, one launch (start us, length us, event | category | flops | bytes accessed | tf_op | source)
XLA Modules:
  0.0 155.8 jit_solution(11920990027239641790)
XLA Ops:
  0.0 1.3 dynamic_slice.3
  1.3 0.8 reshape.3
  2.1 0.7 sort.14
  2.9 0.0 copy-start
  2.9 1.3 gather_fusion
  4.2 1.3 broadcast_add_fusion.energy
  5.4 1.3 broadcast_in_dim.15.vir_row
  6.7 1.6 %broadcast_in_dim.17.vir_col = f32[768,1]{1,0:T(8,128)} reshape(f32[768]{0:T(1024)} %param.8) | data formatting | bytes 6144 | tf_op jit(solution)/shard_map/broadcast_in_dim | solution.py:288
  8.3 7.8 %convert_bitcast_fusion.trans = bf16[4,768,512]{2,1,0:T(8,128)(2,1)} fusion(bf16[1,4,1024,512]{3,2,1,0:T(8,128)(2,1)} %param.5, bf16[1024,768]{1,0:T(8,128)(2,1)} %param.6), kind=kOutput, calls=%fused_computation.3 | convolution fusion | flops 3222798336 | bytes 8912896 | tf_op jit(solution)/shard_map/imp,ma->iap/dot_general | solution.py:242
  16.1 0.0 copy-done
  16.1 133.4 %shard_map.55 = f32[768,2048]{1,0:T(8,128)} custom-call(s32[4]{0:T(128)} %copy-done, f32[4]{0:T(128)} %broadcast_add_fusion.energy, bf16[4,768,512]{2,1,0:T(8,128)(2,1)} %convert_bitcast_fusion.trans, f32[768,1]{1,0:T(8,128)} %broadcast_in_dim.17.vir_col, f32[1,768]{1,0:T(1,128)} %broadcast_in_dim.15.vir_row), custom_call_target="tpu_custom_call" | custom-call | flops 28991029248 | bytes 25165824 | tf_op jit(solution)/shard_map/pallas_call | solution.py:259
  149.5 6.3 %copy.12 = f32[1,1,768,2048]{3,2,1,0:T(8,128)} copy(f32[1,1,768,2048]{3,2,1,0:T(8,128)} %bitcast.12) | data formatting | bytes 12582912
  (2 shorter events, 0.0 us)
Async XLA Ops:
  2.9 13.3 %copy-start = (s32[4]{0:T(128)}, s32[4]{0:T(128)S(1)}, u32[]{:S(2)}) copy-start(s32[4]{0:T(128)S(1)} %get-tuple-element.7.owners) | copy-start | bytes 52

commit v2 on v1

--- a/solution.py
+++ b/solution.py
@@ -65,10 +65,43 @@
         sent.append(copy)
         return copy
 
+    middle = lax.rem(lax.div(g + 1, 2), 2) if n_grp >= 4 else 0
+
+    def place(k):
+        if n_grp < 4 or k % 4 < 2:
+            return k
+        return k + middle * (1 - 2 * (k % 2))
+
+    def slice_of(k):
+        if n_grp < 4 or k % 4 < 2:
+            return flip_grp(k)
+        return flip_grp(k) + middle * (flip_grp(k ^ 1) - flip_grp(k))
+
     a2a = [None]
     for k in range(1, n_grp):
         peer = flip_grp(k)
-        a2a.append(go(remote(trans.at[peer], mine.at[k], a2a_s.at[k], a2a_r.at[k], grp=peer)))
+        a2a.append(remote(trans.at[peer], mine.at[k], a2a_s.at[k], a2a_r.at[k], grp=peer))
+
+    def first_sends():
+        a2a[1].start()
+        if n_grp >= 4:
+            pl.when(middle == 1)(a2a[3].start)
+
+    def second_sends():
+        a2a[1].wait_send()
+        if n_grp >= 4:
+            pl.when(middle == 1)(a2a[3].wait_send)
+            a2a[2].start()
+        for k in range(4, n_grp):
+            go(a2a[k])
+
+    def third_sends():
+        if n_grp >= 4:
+            a2a[2].wait_send()
+
+            a2a[3].start()
+
+    first_sends()
     local = pltpu.make_async_copy(trans.at[g], mine.at[0], local_sem)
     local.start()
     local.wait()
@@ -76,16 +109,20 @@
     near_in, msg_in, own_in = {}, {}, {}
 
     def exchange_near(k):
+        at = place(k)
         if k:
-            a2a[k].wait_recv()
+            arrived = mine.at[at]
+            pltpu.make_async_copy(arrived, arrived, a2a_r.at[at]).wait()
+        if k == 2:
+            pl.when(middle == 0)(third_sends)
         pair = go(remote(
-            mine.at[k, pl.ds(sib_half, half)], sib.at[k], sib_s.at[k], sib_r.at[k], wide=flip(w, 0)
+            mine.at[at, pl.ds(sib_half, half)], sib.at[k], sib_s.at[k], sib_r.at[k], wide=flip(w, 0)
         ))
         for h in range(paths):
             peer = flip(w, step_bit(h, 0))
             rows = pl.ds(pl.multiple_of(my_half + h * rb, 16), rb)
             near_in[k, h, 0] = go(remote(
-                mine.at[k, rows], near.at[k, h, 0], near_s.at[k, h, 0], near_r.at[k, h, 0], wide=peer
+                mine.at[at, rows], near.at[k, h, 0], near_s.at[k, h, 0], near_r.at[k, h, 0], wide=peer
             ))
         pair.wait_recv()
         for h in range(paths):
@@ -112,7 +149,7 @@
     def pick(k, h, t, r, who, unit):
         rows = 32 if rb % 32 == 0 else 16
         at = pl.multiple_of(r * rows, rows)
-        value = mine[k, pl.ds(pl.multiple_of(my_half + h * rb + at, 16), rows), :]
+        value = mine[place(k), pl.ds(pl.multiple_of(my_half + h * rb + at, 16), rows), :]
         first = flip(w, step_bit(h, 0))
         choices = [
             (flip(w, 0), lambda: sib[k, pl.ds(pl.multiple_of(h * rb + at, 16), rows), :]),
@@ -184,10 +221,10 @@
             def _(r):
                 rows = pl.ds(pl.multiple_of(r * tile, tile), tile)
                 straight = lax.dot_general(
-                    mine[k, rows, :], owned[k, s], contract, preferred_element_type=jnp.float32
+                    mine[place(k), rows, :], owned[k, s], contract, preferred_element_type=jnp.float32
                 )
                 turned = lax.dot_general(
-                    owned[k, s, rows, :], mine[k], contract, preferred_element_type=jnp.float32
+                    owned[k, s, rows, :], mine[place(k)], contract, preferred_element_type=jnp.float32
                 )
                 value = 2.0 * straight - turned
                 if k:
@@ -197,6 +234,7 @@
     exchange_near(0)
     for t in range(1, bits):
         exchange_far(0, t)
+    second_sends()
     for k in range(n_grp):
         if k + 1 < n_grp:
             exchange_near(k + 1)
@@ -228,12 +266,15 @@
                 preferred_element_type=jnp.float32,
             )
 
-        columns = pl.ds(pl.multiple_of(flip_grp(k) * pb, 128), pb)
+        columns = pl.ds(pl.multiple_of(slice_of(k) * pb, 128), pb)
         copy = pltpu.make_async_copy(stage.at[k % 2], out.at[:, columns], out_sem.at[k % 2])
         copy.start()
         outs.append(copy)
     for copy in outs[-2:]:
         copy.wait()
+    if n_grp >= 4:
+        pl.when(middle == 1)(a2a[2].wait_send)
+        pl.when(middle == 0)(a2a[3].wait_send)
     for copy in sent:
         copy.wait_send()
 

time: 159 us -> 152 us (0.956)
  Pallas kernels: 133 us -> 128 us
    pallas_call x1, Pallas kernels: 133 us -> 128 us  [shards(): pl.pallas_call(functools.partial(kernel, n_grp, n_wide, slots, paths), ou...]
where the time goes in v2:
time: 152 us; the launch traced here: 150 us
  Pallas kernels  128 us (84%)
  local copies, waits for them, and re-layouts  12.6 us (8%)
  matrix products  7.79 us (5%)
  other arithmetic  2.01 us (1%)
    pallas_call x1, Pallas kernels, shards(): pl.pallas_call(functools.partial(kernel, n_grp, n_wide, slots, paths), ou...  128 us
    dot_general x1, matrix products, shards(): jnp.einsum('imp,ma->iap', half_integrals[0], coeff_virtual, preferred_ele...  7.79 us
    unnamed x3, local copies, waits for them, and re-layouts  6.29 us

profile of v2, /device:TPU:0, one launch (start us, length us, event | category | flops | bytes accessed | tf_op | source)
XLA Modules:
  0.0 150.0 jit_solution(14262771098355039373)
XLA Ops:
  0.0 1.3 dynamic_slice.3
  1.3 0.8 reshape.3
  2.1 0.7 sort.14
  2.9 0.0 copy-start
  2.9 1.3 gather_fusion
  4.2 1.3 broadcast_add_fusion.energy
  5.4 1.3 broadcast_in_dim.15.vir_row
  6.7 1.6 %broadcast_in_dim.17.vir_col = f32[768,1]{1,0:T(8,128)} reshape(f32[768]{0:T(1024)} %param.8) | data formatting | bytes 6144 | tf_op jit(solution)/shard_map/broadcast_in_dim | solution.py:329
  8.3 7.8 %convert_bitcast_fusion.trans = bf16[4,768,512]{2,1,0:T(8,128)(2,1)} fusion(bf16[1,4,1024,512]{3,2,1,0:T(8,128)(2,1)} %param.5, bf16[1024,768]{1,0:T(8,128)(2,1)} %param.6), kind=kOutput, calls=%fused_computation.3 | convolution fusion | flops 3222798336 | bytes 8912896 | tf_op jit(solution)/shard_map/imp,ma->iap/dot_general | solution.py:283
  16.1 0.0 copy-done
  16.1 127.6 %shard_map.55 = f32[768,2048]{1,0:T(8,128)} custom-call(s32[4]{0:T(128)} %copy-done, f32[4]{0:T(128)} %broadcast_add_fusion.energy, bf16[4,768,512]{2,1,0:T(8,128)(2,1)} %convert_bitcast_fusion.trans, f32[768,1]{1,0:T(8,128)} %broadcast_in_dim.17.vir_col, f32[1,768]{1,0:T(1,128)} %broadcast_in_dim.15.vir_row), custom_call_target="tpu_custom_call" | custom-call | flops 28991029248 | bytes 25165824 | tf_op jit(solution)/shard_map/pallas_call | solution.py:300
  143.8 6.3 %copy.12 = f32[1,1,768,2048]{3,2,1,0:T(8,128)} copy(f32[1,1,768,2048]{3,2,1,0:T(8,128)} %bitcast.12) | data formatting | bytes 12582912
  (2 shorter events, 0.0 us)
Async XLA Ops:
  2.9 13.3 %copy-start = (s32[4]{0:T(128)}, s32[4]{0:T(128)S(1)}, u32[]{:S(2)}) copy-start(s32[4]{0:T(128)S(1)} %get-tuple-element.7.owners) | copy-start | bytes 52

commit v3 on v2

--- a/solution.py
+++ b/solution.py
@@ -12,10 +12,10 @@
 
 def kernel(
     n_grp, n_wide, slots, paths,
-    owners, energy, trans, vir_col, vir_row,
-    out,
-    mine, sib, near, msg, far, owned, acc, comb, stage,
-    local_sem, a2a_s, a2a_r, sib_s, sib_r, near_s, near_r, msg_s, msg_r, own_s, own_r, out_sem,
+    plan, occ, vir, coeff, half_integrals,
+    comb_out, owned_out,
+    mine, sib, near, msg, far, owned, acc, comb, trans, taken, coeff_t, vir_col,
+    taken_sem, a2a_s, a2a_r, sib_s, sib_r, near_s, near_r, msg_s, msg_r, own_s, own_r, owned_sem, comb_sem,
 ):
     g = lax.axis_index("grp")
     w = lax.axis_index("wide")
@@ -47,6 +47,15 @@
             device_id=device, device_id_type=MESH,
         )
 
+    order = [0, 1, 3, 2] if n_grp >= 4 else [0, 1]
+    order = order + list(range(len(order), n_grp))
+
+    def take(i):
+        return pltpu.make_async_copy(
+            half_integrals.at[0, flip_grp(order[i])], taken.at[i % 2], taken_sem.at[i % 2]
+        )
+
+    take(0).start()
     barrier = pltpu.get_barrier_semaphore()
     for bit in range(bits + 1):
         pl.semaphore_signal(
@@ -56,6 +65,34 @@
         pl.semaphore_signal(
             barrier, inc=1, device_id={"grp": flip_grp(k)}, device_id_type=MESH
         )
+
+    owners = [plan[a, b] for a in range(plan.shape[0]) for b in range(plan.shape[1])]
+    for last in range(slots - 1, 0, -1):
+        for a in range(last):
+            low = jnp.minimum(owners[a], owners[a + 1])
+            owners[a + 1] = jnp.maximum(owners[a], owners[a + 1])
+            owners[a] = low
+
+    tile = 256 if virt % 256 == 0 else virt
+
+    @pl.loop(0, virt // 128)
+    def _(c):
+        columns = pl.ds(pl.multiple_of(c * 128, 128), 128)
+        coeff_t[columns, :] = coeff[:, columns].T
+
+    def transform(i, rows_of):
+        if i + 1 < n_grp:
+            take(i + 1).start()
+        take(i).wait()
+
+        @pl.loop(0, virt // tile)
+        def _(r):
+            rows = pl.ds(pl.multiple_of(r * tile, tile), tile)
+            rows_of[rows, :] = jnp.dot(
+                coeff_t[rows, :], taken[i % 2], preferred_element_type=jnp.float32
+            ).astype(jnp.bfloat16)
+
+    transform(0, mine.at[0])
     pl.semaphore_wait(barrier, bits + n_grp)
 
     sent = []
@@ -80,12 +117,7 @@
     a2a = [None]
     for k in range(1, n_grp):
         peer = flip_grp(k)
-        a2a.append(remote(trans.at[peer], mine.at[k], a2a_s.at[k], a2a_r.at[k], grp=peer))
-
-    def first_sends():
-        a2a[1].start()
-        if n_grp >= 4:
-            pl.when(middle == 1)(a2a[3].start)
+        a2a.append(remote(trans.at[k], mine.at[k], a2a_s.at[k], a2a_r.at[k], grp=peer))
 
     def second_sends():
         a2a[1].wait_send()
@@ -101,21 +133,16 @@
 
             a2a[3].start()
 
-    first_sends()
-    local = pltpu.make_async_copy(trans.at[g], mine.at[0], local_sem)
-    local.start()
-    local.wait()
-
     near_in, msg_in, own_in = {}, {}, {}
 
-    def exchange_near(k):
+    def start_near(k):
         at = place(k)
         if k:
             arrived = mine.at[at]
             pltpu.make_async_copy(arrived, arrived, a2a_r.at[at]).wait()
         if k == 2:
             pl.when(middle == 0)(third_sends)
-        pair = go(remote(
+        near_in[k] = go(remote(
             mine.at[at, pl.ds(sib_half, half)], sib.at[k], sib_s.at[k], sib_r.at[k], wide=flip(w, 0)
         ))
         for h in range(paths):
@@ -124,7 +151,9 @@
             near_in[k, h, 0] = go(remote(
                 mine.at[at, rows], near.at[k, h, 0], near_s.at[k, h, 0], near_r.at[k, h, 0], wide=peer
             ))
-        pair.wait_recv()
+
+    def finish_near(k):
+        near_in[k].wait_recv()
         for h in range(paths):
             peer = flip(w, step_bit(h, 0))
             near_in[k, h, 1] = go(remote(
@@ -209,11 +238,15 @@
         part = owned.at[k, :, pl.ds(my_half, half), :]
         own_in[k] = go(remote(part, part, own_s.at[k], own_r.at[k], wide=flip(w, 0)))
 
-    tile = 256 if virt % 256 == 0 else virt
     contract = (((1,), (1,)), ((), ()))
 
     def intersect(k):
         own_in[k].wait_recv()
+        columns = pl.ds(pl.multiple_of(slice_of(k) * pb, 128), pb)
+        outs.append(pltpu.make_async_copy(
+            owned.at[k], owned_out.at[:, :, columns], owned_sem.at[k]
+        ))
+        outs[-1].start()
 
         @pl.loop(0, slots)
         def _(s):
@@ -231,13 +264,28 @@
                     value = value + acc[s, rows, :]
                 acc[s, rows, :] = value
 
-    exchange_near(0)
+    outs = []
+    start_near(0)
+    transform(1, trans.at[1])
+    a2a[1].start()
+    finish_near(0)
+    for i in range(2, n_grp):
+        transform(i, trans.at[order[i]])
+        if order[i] == 3:
+            pl.when(middle == 1)(a2a[3].start)
+
+    @pl.loop(0, virt // 128)
+    def _(c):
+        part = pl.ds(pl.multiple_of(c * 128, 128), 128)
+        vir_col[part, :] = jnp.broadcast_to(vir[part].reshape(1, 128), (128, 128)).T
+
     for t in range(1, bits):
         exchange_far(0, t)
     second_sends()
     for k in range(n_grp):
         if k + 1 < n_grp:
-            exchange_near(k + 1)
+            start_near(k + 1)
+            finish_near(k + 1)
         to_sibling(k)
         if k + 1 < n_grp:
             for t in range(1, bits):
@@ -245,32 +293,18 @@
         intersect(k)
 
     for s in range(slots):
-        total = energy[s]
+        total = occ[g, w] + occ[g, owners[s]]
+        part = pl.ds(s * virt, virt)
 
         @pl.loop(0, virt // tile)
         def _(r):
             rows = pl.ds(pl.multiple_of(r * tile, tile), tile)
-            denominator = (total - vir_col[rows, :]) - vir_row[...]
-            comb[rows, pl.ds(s * virt, virt)] = (acc[s, rows, :] / denominator).astype(jnp.bfloat16)
-
-    outs = []
-    for k in range(n_grp):
-        if k >= 2:
-            outs[k - 2].wait()
-
-        @pl.loop(0, virt // tile)
-        def _(r):
-            rows = pl.ds(pl.multiple_of(r * tile, tile), tile)
-            stage[k % 2, rows, :] = jnp.dot(
-                comb[rows, :], owned[k].reshape(slots * virt, pb),
-                preferred_element_type=jnp.float32,
-            )
-
-        columns = pl.ds(pl.multiple_of(slice_of(k) * pb, 128), pb)
-        copy = pltpu.make_async_copy(stage.at[k % 2], out.at[:, columns], out_sem.at[k % 2])
-        copy.start()
-        outs.append(copy)
-    for copy in outs[-2:]:
+            denominator = (total - vir_col[rows, :1]) - vir[...].reshape(1, virt)
+            comb[rows, part] = (acc[s, rows, :] / denominator).astype(jnp.bfloat16)
+
+        outs.append(pltpu.make_async_copy(comb.at[:, part], comb_out.at[:, part], comb_sem.at[s]))
+        outs[-1].start()
+    for copy in outs:
         copy.wait()
     if n_grp >= 4:
         pl.when(middle == 1)(a2a[2].wait_send)
@@ -280,14 +314,9 @@
 
 
 def shards(n_grp, n_wide, half_integrals, coeff_virtual, occ_energy, vir_energy, plan):
-    trans = jnp.einsum(
-        "imp,ma->iap", half_integrals[0], coeff_virtual, preferred_element_type=jnp.float32
-    ).astype(jnp.bfloat16)
-    virt, pb = trans.shape[1:]
-    owners = jnp.sort(plan.reshape(-1))
-    slots = owners.shape[0]
-    orbital = lax.axis_index("grp")
-    energy = occ_energy[lax.axis_index("wide"), orbital] + occ_energy[owners, orbital]
+    basis, virt = coeff_virtual.shape
+    pb = half_integrals.shape[3]
+    slots = plan.size
     bits = n_wide.bit_length() - 2
     paths = bits if virt % (32 * bits) == 0 else 1
     rb = virt // 2 // paths
@@ -296,12 +325,15 @@
     smem = pl.BlockSpec(memory_space=pltpu.SMEM)
     vmem = pl.BlockSpec(memory_space=pltpu.VMEM)
     hbm = pl.BlockSpec(memory_space=pl.ANY)
-    flops = 3 * 2 * slots * virt * virt * pb * n_grp
-    density = pl.pallas_call(
+    flops = 2 * 2 * slots * virt * virt * pb * n_grp
+    comb, owned = pl.pallas_call(
         functools.partial(kernel, n_grp, n_wide, slots, paths),
-        out_shape=jax.ShapeDtypeStruct((virt, pb * n_grp), f32),
-        in_specs=[smem, smem, hbm, vmem, vmem],
-        out_specs=hbm,
+        out_shape=[
+            jax.ShapeDtypeStruct((virt, slots * virt), bf16),
+            jax.ShapeDtypeStruct((slots, virt, n_grp * pb), bf16),
+        ],
+        in_specs=[smem, smem, vmem, vmem, hbm],
+        out_specs=[hbm, hbm],
         scratch_shapes=[
             pltpu.VMEM((n_grp, virt, pb), bf16),
             pltpu.VMEM((n_grp, virt // 2, pb), bf16),
@@ -311,14 +343,17 @@
             pltpu.VMEM((n_grp, slots, virt, pb), bf16),
             pltpu.VMEM((slots, virt, virt), f32),
             pltpu.VMEM((virt, slots * virt), bf16),
-            pltpu.VMEM((2, virt, pb), f32),
-            dma(()),
+            pltpu.VMEM((n_grp, virt, pb), bf16),
+            pltpu.VMEM((2, basis, pb), bf16),
+            pltpu.VMEM((virt, basis), bf16),
+            pltpu.VMEM((virt, 128), f32),
+            dma((2,)),
             dma((n_grp,)), dma((n_grp,)),
             dma((n_grp,)), dma((n_grp,)),
             dma((n_grp, paths, 2)), dma((n_grp, paths, 2)),
             dma((n_grp, paths, bits - 1)), dma((n_grp, paths, bits - 1)),
             dma((n_grp,)), dma((n_grp,)),
-            dma((2,)),
+            dma((n_grp,)), dma((slots,)),
         ],
         compiler_params=pltpu.CompilerParams(
             collective_id=0, has_side_effects=True, vmem_limit_bytes=63 * 1024 * 1024
@@ -326,7 +361,10 @@
         cost_estimate=pl.CostEstimate(
             flops=flops, bytes_accessed=16 * virt * pb * n_grp, transcendentals=0
         ),
-    )(owners, energy, trans, vir_energy[:, None], vir_energy[None, :])
+    )(plan, occ_energy.T, vir_energy, coeff_virtual, half_integrals)
+    density = jnp.dot(
+        comb, owned.reshape(slots * virt, n_grp * pb), preferred_element_type=jnp.float32
+    )
     return density[None, None]
 
 

time: 152 us -> 140 us (0.921)
  the two profiles are of different devices: /device:TPU:0 before, /device:TPU:9 now
where the time goes in v3:
time: 140 us
  Pallas kernels  124 us (89%)
  matrix products  15.9 us (11%)
    pallas_call x1, Pallas kernels, shards(): pl.pallas_call(functools.partial(kernel, n_grp, n_wide, slots, paths), ou...  124 us
    dot_general x1, matrix products, shards(): jnp.dot(comb, owned.reshape(slots * virt, n_grp * pb), preferred_element_...  15.9 us

profile of v3, /device:TPU:9, one launch (start us, length us, event | category | flops | bytes accessed | tf_op | source)
XLA Modules:
  0.0 140.2 jit_solution(8254344227838827258)
XLA Ops:
  0.0 124.3 %shard_map.55 = (bf16[768,3072]{1,0:T(8,128)(2,1)}, bf16[4,768,2048]{2,1,0:T(8,128)(2,1)}) custom-call(s32[2,2]{1,0:T(2,128)} %plan.1, f32[4,8]{1,0:T(4,128)} %bitcast.6, f32[768]{0:T(1024)} %vir.1, bf16[1024,768]{1,0:T(8,128)(2,1)} %coeff.1, bf16[1,4,1024,512]{3,2,1,0:T(8,128)(2,1)} %half_integrals.1), custom_call_target="tpu_custom_call" | custom-call | flops 19327352832 | bytes 25165824 | tf_op jit(solution)/shard_map/pallas_call | solution.py:329
  124.3 15.9 %convolution_bitcast_fusion = f32[1,1,768,2048]{3,2,1,0:T(8,128)} fusion(bf16[768,3072]{1,0:T(8,128)(2,1)} %get-tuple-element.7, bf16[3072,2048]{1,0:T(8,128)(2,1)} %bitcast.7), kind=kOutput, calls=%fused_computation | convolution fusion | flops 9663676416 | bytes 23592960 | tf_op jit(solution)/shard_map/dot_general | solution.py:365

commit v4 on v3

--- a/solution.py
+++ b/solution.py
@@ -85,11 +85,13 @@
             take(i + 1).start()
         take(i).wait()
 
-        @pl.loop(0, virt // tile)
+        wide_tile = 256 if pb % 256 == 0 else pb
+
+        @pl.loop(0, pb // wide_tile)
         def _(r):
-            rows = pl.ds(pl.multiple_of(r * tile, tile), tile)
-            rows_of[rows, :] = jnp.dot(
-                coeff_t[rows, :], taken[i % 2], preferred_element_type=jnp.float32
+            columns = pl.ds(pl.multiple_of(r * wide_tile, wide_tile), wide_tile)
+            rows_of[:, columns] = jnp.dot(
+                coeff_t[...], taken[i % 2, :, columns], preferred_element_type=jnp.float32
             ).astype(jnp.bfloat16)
 
     transform(0, mine.at[0])
@@ -240,29 +242,32 @@
 
     contract = (((1,), (1,)), ((), ()))
 
-    def intersect(k):
-        own_in[k].wait_recv()
-        columns = pl.ds(pl.multiple_of(slice_of(k) * pb, 128), pb)
-        outs.append(pltpu.make_async_copy(
-            owned.at[k], owned_out.at[:, :, columns], owned_sem.at[k]
-        ))
-        outs[-1].start()
-
-        @pl.loop(0, slots)
+    def intersect(k, lowest, highest):
+        if lowest == 0:
+            own_in[k].wait_recv()
+            columns = pl.ds(pl.multiple_of(slice_of(k) * pb, 128), pb)
+            outs.append(pltpu.make_async_copy(
+                owned.at[k], owned_out.at[:, :, columns], owned_sem.at[k]
+            ))
+            outs[-1].start()
+
+        @pl.loop(lowest, highest)
         def _(s):
             @pl.loop(0, virt // tile)
             def _(r):
-                rows = pl.ds(pl.multiple_of(r * tile, tile), tile)
+                part = pl.ds(pl.multiple_of(r * tile, tile), tile)
                 straight = lax.dot_general(
-                    mine[place(k), rows, :], owned[k, s], contract, preferred_element_type=jnp.float32
+                    mine[place(k)], owned[k, s, part, :], contract,
+                    preferred_element_type=jnp.float32,
                 )
                 turned = lax.dot_general(
-                    owned[k, s, rows, :], mine[place(k)], contract, preferred_element_type=jnp.float32
+                    owned[k, s], mine[place(k), part, :], contract,
+                    preferred_element_type=jnp.float32,
                 )
                 value = 2.0 * straight - turned
                 if k:
-                    value = value + acc[s, rows, :]
-                acc[s, rows, :] = value
+                    value = value + acc[s, :, part]
+                acc[s, :, part] = value
 
     outs = []
     start_near(0)
@@ -282,15 +287,21 @@
     for t in range(1, bits):
         exchange_far(0, t)
     second_sends()
+    cut = slots // 2
     for k in range(n_grp):
-        if k + 1 < n_grp:
+        last = k + 1 == n_grp
+        if k:
+            intersect(k - 1, 0, slots if last else cut)
+        if not last:
             start_near(k + 1)
             finish_near(k + 1)
         to_sibling(k)
-        if k + 1 < n_grp:
+        if k and not last:
+            intersect(k - 1, cut, slots)
+        if not last:
             for t in range(1, bits):
                 exchange_far(k + 1, t)
-        intersect(k)
+    intersect(n_grp - 1, 0, slots)
 
     for s in range(slots):
         total = occ[g, w] + occ[g, owners[s]]

time: 140 us -> 141 us (level)
  no operation moved by 1% of the time
where the time goes in v4:
time: 141 us; the launch traced here: 140 us
  Pallas kernels  125 us (89%)
  matrix products  15.9 us (11%)
    pallas_call x1, Pallas kernels, shards(): pl.pallas_call(functools.partial(kernel, n_grp, n_wide, slots, paths), ou...  125 us
    dot_general x1, matrix products, shards(): jnp.dot(comb, owned.reshape(slots * virt, n_grp * pb), preferred_element_...  15.9 us

profile of v4, /device:TPU:9, one launch (start us, length us, event | category | flops | bytes accessed | tf_op | source)
XLA Modules:
  0.0 140.5 jit_solution(14001734438785111684)
XLA Ops:
  0.0 124.6 %shard_map.55 = (bf16[768,3072]{1,0:T(8,128)(2,1)}, bf16[4,768,2048]{2,1,0:T(8,128)(2,1)}) custom-call(s32[2,2]{1,0:T(2,128)} %plan.1, f32[4,8]{1,0:T(4,128)} %bitcast.6, f32[768]{0:T(1024)} %vir.1, bf16[1024,768]{1,0:T(8,128)(2,1)} %coeff.1, bf16[1,4,1024,512]{3,2,1,0:T(8,128)(2,1)} %half_integrals.1), custom_call_target="tpu_custom_call" | custom-call | flops 19327352832 | bytes 25165824 | tf_op jit(solution)/shard_map/pallas_call | solution.py:340
  124.6 15.9 %convolution_bitcast_fusion = f32[1,1,768,2048]{3,2,1,0:T(8,128)} fusion(bf16[768,3072]{1,0:T(8,128)(2,1)} %get-tuple-element.7, bf16[3072,2048]{1,0:T(8,128)(2,1)} %bitcast.7), kind=kOutput, calls=%fused_computation | convolution fusion | flops 9663676416 | bytes 23592960 | tf_op jit(solution)/shard_map/dot_general | solution.py:376

commit v5 on v3

--- a/solution.py
+++ b/solution.py
@@ -11,7 +11,7 @@
 
 
 def kernel(
-    n_grp, n_wide, slots, paths,
+    n_grp, n_wide, slots, paths, n_sub,
     plan, occ, vir, coeff, half_integrals,
     comb_out, owned_out,
     mine, sib, near, msg, far, owned, acc, comb, trans, taken, coeff_t, vir_col,
@@ -20,6 +20,7 @@
     g = lax.axis_index("grp")
     w = lax.axis_index("wide")
     virt, pb = mine.shape[1], mine.shape[2]
+    n_parts = n_grp * n_sub
     half = virt // 2
     rb = half // paths
     bits = n_wide.bit_length() - 2
@@ -85,14 +86,13 @@
             take(i + 1).start()
         take(i).wait()
 
-        @pl.loop(0, virt // tile)
-        def _(r):
-            rows = pl.ds(pl.multiple_of(r * tile, tile), tile)
-            rows_of[rows, :] = jnp.dot(
-                coeff_t[rows, :], taken[i % 2], preferred_element_type=jnp.float32
+        for c in range(n_sub):
+            rows_of[order[i] * n_sub + c] = jnp.dot(
+                coeff_t[...], taken[i % 2, :, c * pb:(c + 1) * pb],
+                preferred_element_type=jnp.float32,
             ).astype(jnp.bfloat16)
 
-    transform(0, mine.at[0])
+    transform(0, mine)
     pl.semaphore_wait(barrier, bits + n_grp)
 
     sent = []
@@ -104,43 +104,51 @@
 
     middle = lax.rem(lax.div(g + 1, 2), 2) if n_grp >= 4 else 0
 
-    def place(k):
+    def place(j):
+        if n_grp < 4 or j // n_sub % 4 < 2:
+            return j
+        return j + middle * n_sub * (1 - 2 * (j // n_sub % 2))
+
+    def column_of(j):
+        k = j // n_sub
         if n_grp < 4 or k % 4 < 2:
-            return k
-        return k + middle * (1 - 2 * (k % 2))
-
-    def slice_of(k):
-        if n_grp < 4 or k % 4 < 2:
-            return flip_grp(k)
-        return flip_grp(k) + middle * (flip_grp(k ^ 1) - flip_grp(k))
-
-    a2a = [None]
-    for k in range(1, n_grp):
-        peer = flip_grp(k)
-        a2a.append(remote(trans.at[k], mine.at[k], a2a_s.at[k], a2a_r.at[k], grp=peer))
+            index = flip_grp(k)
+        else:
+            index = flip_grp(k) + middle * (flip_grp(k ^ 1) - flip_grp(k))
+        return pl.multiple_of(index * (n_sub * pb) + j % n_sub * pb, 128)
+
+    def a2a(k):
+        for j in range(k * n_sub, (k + 1) * n_sub):
+            yield remote(trans.at[j], mine.at[j], a2a_s.at[j], a2a_r.at[j], grp=flip_grp(k))
+
+    def send(k):
+        for copy in a2a(k):
+            copy.start()
+
+    def wait_sent(k):
+        for copy in a2a(k):
+            copy.wait_send()
 
     def second_sends():
-        a2a[1].wait_send()
+        wait_sent(1)
         if n_grp >= 4:
-            pl.when(middle == 1)(a2a[3].wait_send)
-            a2a[2].start()
+            pl.when(middle == 1)(lambda: wait_sent(3))
+            send(2)
         for k in range(4, n_grp):
-            go(a2a[k])
+            send(k)
 
     def third_sends():
-        if n_grp >= 4:
-            a2a[2].wait_send()
-
-            a2a[3].start()
+        wait_sent(2)
+        send(3)
 
     near_in, msg_in, own_in = {}, {}, {}
 
     def start_near(k):
         at = place(k)
-        if k:
+        if k >= n_sub:
             arrived = mine.at[at]
             pltpu.make_async_copy(arrived, arrived, a2a_r.at[at]).wait()
-        if k == 2:
+        if n_grp >= 4 and k == 3 * n_sub - 1:
             pl.when(middle == 0)(third_sends)
         near_in[k] = go(remote(
             mine.at[at, pl.ds(sib_half, half)], sib.at[k], sib_s.at[k], sib_r.at[k], wide=flip(w, 0)
@@ -240,57 +248,79 @@
 
     contract = (((1,), (1,)), ((), ()))
 
-    def intersect(k):
+    def store_rows(k):
         own_in[k].wait_recv()
-        columns = pl.ds(pl.multiple_of(slice_of(k) * pb, 128), pb)
         outs.append(pltpu.make_async_copy(
-            owned.at[k], owned_out.at[:, :, columns], owned_sem.at[k]
+            owned.at[k], owned_out.at[:, :, pl.ds(column_of(k), pb)], owned_sem.at[k]
         ))
         outs[-1].start()
 
-        @pl.loop(0, slots)
+    def intersect(parts, lowest, highest):
+        @pl.loop(lowest, highest)
         def _(s):
             @pl.loop(0, virt // tile)
             def _(r):
-                rows = pl.ds(pl.multiple_of(r * tile, tile), tile)
-                straight = lax.dot_general(
-                    mine[place(k), rows, :], owned[k, s], contract, preferred_element_type=jnp.float32
-                )
-                turned = lax.dot_general(
-                    owned[k, s, rows, :], mine[place(k)], contract, preferred_element_type=jnp.float32
-                )
-                value = 2.0 * straight - turned
-                if k:
-                    value = value + acc[s, rows, :]
-                acc[s, rows, :] = value
+                part = pl.ds(pl.multiple_of(r * tile, tile), tile)
+                value = None if parts[0] == 0 else acc[s, :, part]
+                for j in parts:
+                    straight = lax.dot_general(
+                        mine[place(j)], owned[j, s, part, :], contract,
+                        preferred_element_type=jnp.float32,
+                    )
+                    turned = lax.dot_general(
+                        owned[j, s], mine[place(j), part, :], contract,
+                        preferred_element_type=jnp.float32,
+                    )
+                    term = 2.0 * straight - turned
+                    value = term if value is None else value + term
+                acc[s, :, part] = value
 
     outs = []
     start_near(0)
-    transform(1, trans.at[1])
-    a2a[1].start()
+    transform(1, trans)
+    send(1)
     finish_near(0)
     for i in range(2, n_grp):
-        transform(i, trans.at[order[i]])
+        transform(i, trans)
         if order[i] == 3:
-            pl.when(middle == 1)(a2a[3].start)
+            pl.when(middle == 1)(lambda: send(3))
 
     @pl.loop(0, virt // 128)
     def _(c):
         part = pl.ds(pl.multiple_of(c * 128, 128), 128)
         vir_col[part, :] = jnp.broadcast_to(vir[part].reshape(1, 128), (128, 128)).T
 
-    for t in range(1, bits):
-        exchange_far(0, t)
-    second_sends()
-    for k in range(n_grp):
-        if k + 1 < n_grp:
-            start_near(k + 1)
-            finish_near(k + 1)
-        to_sibling(k)
-        if k + 1 < n_grp:
-            for t in range(1, bits):
-                exchange_far(k + 1, t)
-        intersect(k)
+    cut = slots // 2
+    todo = []
+    for j in range(n_parts):
+        if j + 1 < n_parts:
+            if j + 1 == 2 * n_sub - 1:
+                second_sends()
+            start_near(j + 1)
+            finish_near(j + 1)
+        for t in range(1, bits):
+            exchange_far(j, t)
+        if j:
+            to_sibling(j - 1)
+        if j >= 2:
+            store_rows(j - 2)
+            if (j - 1) % n_sub == 0:
+                parts = list(range(j - 1 - n_sub, j - 1))
+                todo += [(parts, 0, cut), (parts, cut, slots)]
+        for _ in range(2 // n_sub):
+            if todo:
+                intersect(*todo.pop(0))
+    for item in todo:
+        intersect(*item)
+    to_sibling(n_parts - 1)
+    if n_parts >= 2:
+        store_rows(n_parts - 2)
+        if n_sub > 1:
+            intersect(list(range(n_parts - n_sub, n_parts - 1)), 0, slots)
+        else:
+            intersect([n_parts - 2], 0, slots)
+    store_rows(n_parts - 1)
+    intersect([n_parts - 1], 0, slots)
 
     for s in range(slots):
         total = occ[g, w] + occ[g, owners[s]]
@@ -307,15 +337,20 @@
     for copy in outs:
         copy.wait()
     if n_grp >= 4:
-        pl.when(middle == 1)(a2a[2].wait_send)
-        pl.when(middle == 0)(a2a[3].wait_send)
+        pl.when(middle == 1)(lambda: wait_sent(2))
+        pl.when(middle == 0)(lambda: wait_sent(3))
+    for k in range(4, n_grp):
+        wait_sent(k)
     for copy in sent:
         copy.wait_send()
 
 
 def shards(n_grp, n_wide, half_integrals, coeff_virtual, occ_energy, vir_energy, plan):
     basis, virt = coeff_virtual.shape
-    pb = half_integrals.shape[3]
+    aux = half_integrals.shape[3]
+    n_sub = 2 if aux % 512 == 0 else 1
+    pb = aux // n_sub
+    n_parts = n_grp * n_sub
     slots = plan.size
     bits = n_wide.bit_length() - 2
     paths = bits if virt % (32 * bits) == 0 else 1
@@ -325,45 +360,45 @@
     smem = pl.BlockSpec(memory_space=pltpu.SMEM)
     vmem = pl.BlockSpec(memory_space=pltpu.VMEM)
     hbm = pl.BlockSpec(memory_space=pl.ANY)
-    flops = 2 * 2 * slots * virt * virt * pb * n_grp
+    flops = 2 * 2 * slots * virt * virt * aux * n_grp
     comb, owned = pl.pallas_call(
-        functools.partial(kernel, n_grp, n_wide, slots, paths),
+        functools.partial(kernel, n_grp, n_wide, slots, paths, n_sub),
         out_shape=[
             jax.ShapeDtypeStruct((virt, slots * virt), bf16),
-            jax.ShapeDtypeStruct((slots, virt, n_grp * pb), bf16),
+            jax.ShapeDtypeStruct((slots, virt, n_grp * aux), bf16),
         ],
         in_specs=[smem, smem, vmem, vmem, hbm],
         out_specs=[hbm, hbm],
         scratch_shapes=[
-            pltpu.VMEM((n_grp, virt, pb), bf16),
-            pltpu.VMEM((n_grp, virt // 2, pb), bf16),
-            pltpu.VMEM((n_grp, paths, 2, rb, pb), bf16),
-            pltpu.VMEM((n_grp, paths, bits - 1, slots - 1, rb, pb), bf16),
-            pltpu.VMEM((n_grp, paths, bits - 1, slots - 1, rb, pb), bf16),
-            pltpu.VMEM((n_grp, slots, virt, pb), bf16),
+            pltpu.VMEM((n_parts, virt, pb), bf16),
+            pltpu.VMEM((n_parts, virt // 2, pb), bf16),
+            pltpu.VMEM((n_parts, paths, 2, rb, pb), bf16),
+            pltpu.VMEM((n_parts, paths, bits - 1, slots - 1, rb, pb), bf16),
+            pltpu.VMEM((n_parts, paths, bits - 1, slots - 1, rb, pb), bf16),
+            pltpu.VMEM((n_parts, slots, virt, pb), bf16),
             pltpu.VMEM((slots, virt, virt), f32),
             pltpu.VMEM((virt, slots * virt), bf16),
-            pltpu.VMEM((n_grp, virt, pb), bf16),
-            pltpu.VMEM((2, basis, pb), bf16),
+            pltpu.VMEM((n_parts, virt, pb), bf16),
+            pltpu.VMEM((2, basis, aux), bf16),
             pltpu.VMEM((virt, basis), bf16),
             pltpu.VMEM((virt, 128), f32),
             dma((2,)),
-            dma((n_grp,)), dma((n_grp,)),
-            dma((n_grp,)), dma((n_grp,)),
-            dma((n_grp, paths, 2)), dma((n_grp, paths, 2)),
-            dma((n_grp, paths, bits - 1)), dma((n_grp, paths, bits - 1)),
-            dma((n_grp,)), dma((n_grp,)),
-            dma((n_grp,)), dma((slots,)),
+            dma((n_parts,)), dma((n_parts,)),
+            dma((n_parts,)), dma((n_parts,)),
+            dma((n_parts, paths, 2)), dma((n_parts, paths, 2)),
+            dma((n_parts, paths, bits - 1)), dma((n_parts, paths, bits - 1)),
+            dma((n_parts,)), dma((n_parts,)),
+            dma((n_parts,)), dma((slots,)),
         ],
         compiler_params=pltpu.CompilerParams(
             collective_id=0, has_side_effects=True, vmem_limit_bytes=63 * 1024 * 1024
         ),
         cost_estimate=pl.CostEstimate(
-            flops=flops, bytes_accessed=16 * virt * pb * n_grp, transcendentals=0
+            flops=flops, bytes_accessed=16 * virt * aux * n_grp, transcendentals=0
         ),
     )(plan, occ_energy.T, vir_energy, coeff_virtual, half_integrals)
     density = jnp.dot(
-        comb, owned.reshape(slots * virt, n_grp * pb), preferred_element_type=jnp.float32
+        comb, owned.reshape(slots * virt, n_grp * aux), preferred_element_type=jnp.float32
     )
     return density[None, None]
 

time: 140 us -> 138 us (0.986)
  the two profiles are of different devices: /device:TPU:9 before, /device:TPU:0 now
where the time goes in v5:
time: 138 us; the launch traced here: 137 us
  Pallas kernels  121 us (88%)
  matrix products  15.9 us (12%)
    pallas_call x1, Pallas kernels, shards(): pl.pallas_call(functools.partial(kernel, n_grp, n_wide, slots, paths, n_s...  121 us
    dot_general x1, matrix products, shards(): jnp.dot(comb, owned.reshape(slots * virt, n_grp * aux), preferred_element...  15.9 us

profile of v5, /device:TPU:0, one launch (start us, length us, event | category | flops | bytes accessed | tf_op | source)
XLA Modules:
  0.0 137.4 jit_solution(9797294325088580575)
XLA Ops:
  0.0 121.4 %shard_map.55 = (bf16[768,3072]{1,0:T(8,128)(2,1)}, bf16[4,768,2048]{2,1,0:T(8,128)(2,1)}) custom-call(s32[2,2]{1,0:T(2,128)} %plan.1, f32[4,8]{1,0:T(4,128)} %bitcast.6, f32[768]{0:T(1024)} %vir.1, bf16[1024,768]{1,0:T(8,128)(2,1)} %coeff.1, bf16[1,4,1024,512]{3,2,1,0:T(8,128)(2,1)} %half_integrals.1), custom_call_target="tpu_custom_call" | custom-call | flops 19327352832 | bytes 25165824 | tf_op jit(solution)/shard_map/pallas_call | solution.py:364
  121.4 15.9 %convolution_bitcast_fusion = f32[1,1,768,2048]{3,2,1,0:T(8,128)} fusion(bf16[768,3072]{1,0:T(8,128)(2,1)} %get-tuple-element.7, bf16[3072,2048]{1,0:T(8,128)(2,1)} %bitcast.7), kind=kOutput, calls=%fused_computation | convolution fusion | flops 9663676416 | bytes 23592960 | tf_op jit(solution)/shard_map/dot_general | solution.py:400

commit v6 on v5

--- a/solution.py
+++ b/solution.py
@@ -14,7 +14,7 @@
     n_grp, n_wide, slots, paths, n_sub,
     plan, occ, vir, coeff, half_integrals,
     comb_out, owned_out,
-    mine, sib, near, msg, far, owned, acc, comb, trans, taken, coeff_t, vir_col,
+    mine, sib, near, msg, far, owned, acc, comb, trans, taken, coeff_t, vir_col, vir_row,
     taken_sem, a2a_s, a2a_r, sib_s, sib_r, near_s, near_r, msg_s, msg_r, own_s, own_r, owned_sem, comb_sem,
 ):
     g = lax.axis_index("grp")
@@ -255,6 +255,15 @@
         ))
         outs[-1].start()
 
+    def term_of(j, s, part):
+        straight = lax.dot_general(
+            mine[place(j)], owned[j, s, part, :], contract, preferred_element_type=jnp.float32
+        )
+        turned = lax.dot_general(
+            owned[j, s], mine[place(j), part, :], contract, preferred_element_type=jnp.float32
+        )
+        return 2.0 * straight - turned
+
     def intersect(parts, lowest, highest):
         @pl.loop(lowest, highest)
         def _(s):
@@ -263,15 +272,7 @@
                 part = pl.ds(pl.multiple_of(r * tile, tile), tile)
                 value = None if parts[0] == 0 else acc[s, :, part]
                 for j in parts:
-                    straight = lax.dot_general(
-                        mine[place(j)], owned[j, s, part, :], contract,
-                        preferred_element_type=jnp.float32,
-                    )
-                    turned = lax.dot_general(
-                        owned[j, s], mine[place(j), part, :], contract,
-                        preferred_element_type=jnp.float32,
-                    )
-                    term = 2.0 * straight - turned
+                    term = term_of(j, s, part)
                     value = term if value is None else value + term
                 acc[s, :, part] = value
 
@@ -288,6 +289,7 @@
     @pl.loop(0, virt // 128)
     def _(c):
         part = pl.ds(pl.multiple_of(c * 128, 128), 128)
+        vir_row[:, part] = vir[part].reshape(1, 128)
         vir_col[part, :] = jnp.broadcast_to(vir[part].reshape(1, 128), (128, 128)).T
 
     cut = slots // 2
@@ -320,18 +322,20 @@
         else:
             intersect([n_parts - 2], 0, slots)
     store_rows(n_parts - 1)
-    intersect([n_parts - 1], 0, slots)
 
     for s in range(slots):
         total = occ[g, w] + occ[g, owners[s]]
-        part = pl.ds(s * virt, virt)
 
         @pl.loop(0, virt // tile)
         def _(r):
-            rows = pl.ds(pl.multiple_of(r * tile, tile), tile)
-            denominator = (total - vir_col[rows, :1]) - vir[...].reshape(1, virt)
-            comb[rows, part] = (acc[s, rows, :] / denominator).astype(jnp.bfloat16)
-
+            part = pl.ds(pl.multiple_of(r * tile, tile), tile)
+            value = acc[s, :, part] + term_of(n_parts - 1, s, part)
+            denominator = (total - vir_col[:, :1]) - vir_row[:, part]
+            comb[:, pl.ds(pl.multiple_of(s * virt + r * tile, tile), tile)] = (
+                value / denominator
+            ).astype(jnp.bfloat16)
+
+        part = pl.ds(s * virt, virt)
         outs.append(pltpu.make_async_copy(comb.at[:, part], comb_out.at[:, part], comb_sem.at[s]))
         outs[-1].start()
     for copy in outs:
@@ -343,6 +347,13 @@
         wait_sent(k)
     for copy in sent:
         copy.wait_send()
+
+
+def density_kernel(comb, owned, out):
+    slots, virt, columns = owned.shape
+    out[...] = jnp.dot(
+        comb[...], owned[...].reshape(slots * virt, columns), preferred_element_type=jnp.float32
+    )
 
 
 def shards(n_grp, n_wide, half_integrals, coeff_virtual, occ_energy, vir_energy, plan):
@@ -382,6 +393,7 @@
             pltpu.VMEM((2, basis, aux), bf16),
             pltpu.VMEM((virt, basis), bf16),
             pltpu.VMEM((virt, 128), f32),
+            pltpu.VMEM((1, virt), f32),
             dma((2,)),
             dma((n_parts,)), dma((n_parts,)),
             dma((n_parts,)), dma((n_parts,)),
@@ -397,9 +409,23 @@
             flops=flops, bytes_accessed=16 * virt * aux * n_grp, transcendentals=0
         ),
     )(plan, occ_energy.T, vir_energy, coeff_virtual, half_integrals)
-    density = jnp.dot(
-        comb, owned.reshape(slots * virt, n_grp * aux), preferred_element_type=jnp.float32
-    )
+    span = n_grp * aux
+    wide_tile = 256 if span % 256 == 0 else span
+    density = pl.pallas_call(
+        density_kernel,
+        out_shape=jax.ShapeDtypeStruct((virt, span), f32),
+        grid=(span // wide_tile,),
+        in_specs=[
+            pl.BlockSpec((virt, slots * virt), lambda c: (0, 0)),
+            pl.BlockSpec((slots, virt, wide_tile), lambda c: (0, 0, c)),
+        ],
+        out_specs=pl.BlockSpec((virt, wide_tile), lambda c: (0, c)),
+        compiler_params=pltpu.CompilerParams(vmem_limit_bytes=48 * 1024 * 1024),
+        cost_estimate=pl.CostEstimate(
+            flops=2 * slots * virt * virt * span, bytes_accessed=14 * virt * span,
+            transcendentals=0,
+        ),
+    )(comb, owned)
     return density[None, None]
 
 

time: 138 us -> 137 us (level)
  matrix products: 15.9 us -> 0 us
  Pallas kernels: 121 us -> 134 us
  local copies, waits for them, and re-layouts: 0 us -> 2.33 us
    dot_general x1 -> x0, matrix products: 15.9 us -> none  [shards(): jnp.dot(comb, owned.reshape(slots * virt, n_grp * aux), preferred_element...]
    pallas_call x0 -> x1, Pallas kernels: none -> 14.5 us  [shards(): pl.pallas_call(density_kernel, out_shape=jax.ShapeDtypeStruct((virt, span...]
    unnamed x0 -> x2, local copies, waits for them, and re-layouts: none -> 2.33 us
    pallas_call x1, Pallas kernels: 121 us -> 119 us  [shards(): pl.pallas_call(functools.partial(kernel, n_grp, n_wide, slots, paths, n_s...]
where the time goes in v6:
time: 137 us; the launch traced here: 136 us
  Pallas kernels  134 us (98%)
  local copies, waits for them, and re-layouts  2.33 us (2%)
    pallas_call x1, Pallas kernels, shards(): pl.pallas_call(functools.partial(kernel, n_grp, n_wide, slots, paths, n_s...  119 us
    pallas_call x1, Pallas kernels, shards(): pl.pallas_call(density_kernel, out_shape=jax.ShapeDtypeStruct((virt, span...  14.5 us

profile of v6, /device:TPU:0, one launch (start us, length us, event | category | flops | bytes accessed | tf_op | source)
XLA Modules:
  0.0 136.3 jit_solution(1319911308838301982)
XLA Ops:
  0.0 119.4 %shard_map.55 = (bf16[768,3072]{1,0:T(8,128)(2,1)}, bf16[4,768,2048]{2,1,0:T(8,128)(2,1)}) custom-call(s32[2,2]{1,0:T(2,128)} %plan.1, f32[4,8]{1,0:T(4,128)} %bitcast.2, f32[768]{0:T(1024)} %vir.1, bf16[1024,768]{1,0:T(8,128)(2,1)} %coeff.1, bf16[1,4,1024,512]{3,2,1,0:T(8,128)(2,1)} %half_integrals.1), custom_call_target="tpu_custom_call" | custom-call | flops 19327352832 | bytes 25165824 | tf_op jit(solution)/shard_map/pallas_call | solution.py:375
  119.4 0.0 copy-start
  119.4 2.3 %copy-done = bf16[768,3072]{1,0:T(8,128)(2,1)S(1)} copy-done((bf16[768,3072]{1,0:T(8,128)(2,1)S(1)}, bf16[768,3072]{1,0:T(8,128)(2,1)}, u32[]{:S(2)}) %copy-start) | copy-done | bytes 4718616
  121.8 14.5 %shard_map.56 = f32[768,2048]{1,0:T(8,128)} custom-call(bf16[768,3072]{1,0:T(8,128)(2,1)S(1)} %copy-done, bf16[4,768,2048]{2,1,0:T(8,128)(2,1)} %get-tuple-element.8.owned), custom_call_target="tpu_custom_call" | custom-call | flops 9663676416 | bytes 22020096 | tf_op jit(solution)/shard_map/pallas_call | solution.py:414
Async XLA Ops:
  119.4 2.3 %copy-start = (bf16[768,3072]{1,0:T(8,128)(2,1)S(1)}, bf16[768,3072]{1,0:T(8,128)(2,1)}, u32[]{:S(2)}) copy-start(bf16[768,3072]{1,0:T(8,128)(2,1)} %get-tuple-element.7.comb) | copy-start | bytes 14155780

commit v7 on v6

--- a/solution.py
+++ b/solution.py
@@ -420,7 +420,7 @@
             pl.BlockSpec((slots, virt, wide_tile), lambda c: (0, 0, c)),
         ],
         out_specs=pl.BlockSpec((virt, wide_tile), lambda c: (0, c)),
-        compiler_params=pltpu.CompilerParams(vmem_limit_bytes=48 * 1024 * 1024),
+        compiler_params=pltpu.CompilerParams(vmem_limit_bytes=63 * 1024 * 1024),
         cost_estimate=pl.CostEstimate(
             flops=2 * slots * virt * virt * span, bytes_accessed=14 * virt * span,
             transcendentals=0,

time: 137 us -> 136 us (level)
  local copies, waits for them, and re-layouts: 2.33 us -> 0 us
    unnamed x2 -> x0, local copies, waits for them, and re-layouts: 2.33 us -> none
    pallas_call x1, Pallas kernels: 14.5 us -> 16 us  [shards(): pl.pallas_call(density_kernel, out_shape=jax.ShapeDtypeStruct((virt, span...]
where the time goes in v7:
time: 136 us; the launch traced here: 135 us
  Pallas kernels  135 us (99%)
    pallas_call x1, Pallas kernels, shards(): pl.pallas_call(functools.partial(kernel, n_grp, n_wide, slots, paths, n_s...  119 us
    pallas_call x1, Pallas kernels, shards(): pl.pallas_call(density_kernel, out_shape=jax.ShapeDtypeStruct((virt, span...  16 us

profile of v7, /device:TPU:0, one launch (start us, length us, event | category | flops | bytes accessed | tf_op | source)
XLA Modules:
  0.0 135.3 jit_solution(11820428680697453654)
XLA Ops:
  0.0 119.4 %shard_map.55 = (bf16[768,3072]{1,0:T(8,128)(2,1)}, bf16[4,768,2048]{2,1,0:T(8,128)(2,1)}) custom-call(s32[2,2]{1,0:T(2,128)} %plan.1, f32[4,8]{1,0:T(4,128)} %bitcast.2, f32[768]{0:T(1024)} %vir.1, bf16[1024,768]{1,0:T(8,128)(2,1)} %coeff.1, bf16[1,4,1024,512]{3,2,1,0:T(8,128)(2,1)} %half_integrals.1), custom_call_target="tpu_custom_call" | custom-call | flops 19327352832 | bytes 25165824 | tf_op jit(solution)/shard_map/pallas_call | solution.py:375
  119.4 16.0 %shard_map.56 = f32[768,2048]{1,0:T(8,128)} custom-call(bf16[768,3072]{1,0:T(8,128)(2,1)} %get-tuple-element.7.comb, bf16[4,768,2048]{2,1,0:T(8,128)(2,1)} %get-tuple-element.8.owned), custom_call_target="tpu_custom_call" | custom-call | flops 9663676416 | bytes 22020096 | tf_op jit(solution)/shard_map/pallas_call | solution.py:414
